TPU v7x, 256 devices: a whole 4x4x8 slice. The times are simulated.
256 devices in a mesh: section: 8 (over z), tp: 32 (over x, y, core).
Axes of the slice: x: 4, y: 4, z: 8, core: 2. Of those that a mesh axis runs over, the one named last changes fastest.
Arguments:
- section_inputs: bfloat16 [8, 192, 4096], P('section', None, 'tp'), may hold values from -6 to 6
- top_gradient: float32 [192, 4096], P(None, 'tp'), may hold values from -6 to 6
- gate_weight: bfloat16 [8, 4096, 14336], P('section', None, 'tp'), may hold values from -0.09375 to 0.09375
- up_weight: bfloat16 [8, 4096, 14336], P('section', None, 'tp'), may hold values from -0.09375 to 0.09375
- down_weight: bfloat16 [8, 14336, 4096], P('section', 'tp'), may hold values from -0.046875 to 0.046875
Outputs:
- section_grads: float32 [8, 192, 4096], P('section', None, 'tp')
- kept_scores: float32 [8, 3584, 4096], P('section', 'tp')
All inputs are finite; a program needn't handle non-finite values.
Results may differ from a plain program's by a relative error of at most 0.04.
Values may be sent and summed in bfloat16 or wider, within the bound.
A program may use at most 128 MiB of HBM per device.

v0:
```python
import jax
import jax.numpy as jnp
from jax import lax
from jax.sharding import PartitionSpec as P

SEQ = 64
SAMPLES = 3


def from_behind(value, axis, steps):
    count = lax.axis_size(axis)
    first, last = (max(0, -steps), min(count, count - steps))
    return lax.ppermute(value, axis, [(source, source + steps) for source in range(first, last)])


def shards(section_inputs, top_gradient, gate_weight, up_weight, down_weight):
    sections = lax.axis_size("section")
    position = lax.axis_index("section")
    local_inputs = section_inputs[0]
    w_gate = gate_weight[0]
    w_up = up_weight[0]
    w_down = down_weight[0]
    total_rows = local_inputs.shape[0]
    shard_width = local_inputs.shape[1]
    hidden_cols = w_gate.shape[1]
    model_width = w_down.shape[1]
    piece = lax.all_gather(local_inputs, "tp", axis=1, tiled=True)
    pre_gate = jnp.dot(piece, w_gate, preferred_element_type=jnp.float32)
    pre_up = jnp.dot(piece, w_up, preferred_element_type=jnp.float32)
    silu_gate = jax.nn.silu(pre_gate)
    hidden = (silu_gate * pre_up).astype(jnp.bfloat16)
    sigmoid_gate = jax.nn.sigmoid(pre_gate)
    gate_factor = pre_up * (sigmoid_gate * (1.0 + pre_gate * (1.0 - sigmoid_gate)))
    micro = 1
    block_rows = total_rows // micro
    ticks = sections + micro - 1
    contract = (((1,), (1,)), ((), ()))

    def backward(full_grad, start):
        hidden_grad = lax.dot_general(
            full_grad, w_down, contract, preferred_element_type=jnp.float32
        )
        grad_gate = (hidden_grad * gate_factor).astype(jnp.bfloat16)
        grad_up = (hidden_grad * silu_gate).astype(jnp.bfloat16)
        return lax.dot_general(
            grad_gate, w_gate, contract, preferred_element_type=jnp.float32
        ) + lax.dot_general(grad_up, w_up, contract, preferred_element_type=jnp.float32)

    def skipped(full_grad, start):
        return jnp.zeros((block_rows, model_width), jnp.float32)

    def advance(step_index, carry):
        incoming, section_grad, seen_grad = carry
        micro_index = step_index - (sections - 1 - position)
        active = jnp.logical_and(micro_index >= 0, micro_index < micro)
        start = jnp.clip(micro_index, 0, micro - 1) * block_rows
        grad_in = jnp.where(position == sections - 1, top_gradient, incoming)
        full_grad = lax.all_gather(grad_in.astype(jnp.bfloat16), "tp", axis=1, tiled=True)
        partial_term = lax.cond(active, backward, skipped, full_grad, start)
        input_term = lax.psum_scatter(
            partial_term.astype(jnp.bfloat16), "tp", scatter_dimension=1, tiled=True
        ).astype(jnp.float32)
        result = grad_in + input_term
        section_grad = jnp.where(active, result, section_grad)
        seen_grad = jnp.where(active, full_grad, seen_grad)
        incoming = from_behind(result.astype(jnp.bfloat16), "section", -1).astype(result.dtype)
        return (incoming, section_grad, seen_grad)

    initial = (
        jnp.zeros((block_rows, shard_width), jnp.float32),
        jnp.zeros((total_rows, shard_width), jnp.float32),
        jnp.zeros((total_rows, model_width), jnp.bfloat16),
    )
    leftover, section_grad, seen_grad = lax.fori_loop(0, ticks, advance, initial)
    squares = jnp.zeros((hidden_cols, model_width), jnp.float32)
    for sample in range(SAMPLES):
        hidden_rows = hidden[sample * SEQ : (sample + 1) * SEQ]
        grad_rows = seen_grad[sample * SEQ : (sample + 1) * SEQ]
        weight_grad = lax.dot_general(
            hidden_rows, grad_rows, (((0,), (0,)), ((), ())), preferred_element_type=jnp.float32
        )
        squares = squares + weight_grad * weight_grad
    score = jnp.abs(w_down.astype(jnp.float32)) * jnp.sqrt(squares)
    ordered = jnp.sort(score.reshape(hidden_cols // 4, 4, model_width), axis=1)
    kept = ordered[:, 2] + ordered[:, 3]
    return (section_grad[None], kept[None])


def solution(mesh):
    in_specs = (
        P("section", None, "tp"),
        P(None, "tp"),
        P("section", None, "tp"),
        P("section", None, "tp"),
        P("section", "tp", None),
    )
    out_specs = (P("section", None, "tp"), P("section", "tp", None))
    return jax.shard_map(shards, mesh=mesh, in_specs=in_specs, out_specs=out_specs, check_vma=False)
```

profile of v0, /device:TPU:1, one launch (start us, length us, event | category | flops | bytes accessed | tf_op | source)
XLA Modules:
  0.0 1424.5 jit_solution(12751484454029844301)
XLA Ops:
  7.9 6.4 copy.13
  14.4 6.5 copy.12
  20.8 42.7 %all-gather.4.cloned.1.call-done = bf16[1,192,4096]{2,1,0:T(8,128)(2,1)} async-done(((bf16[1,192,128]{2,1,0:T(8,128)(2,1)}), bf16[1,192,4096]{2,1,0:T(8,128)(2,1)}) %all-gather.4.cloned.1.call-update) | async-done | bytes 1572880 | tf_op jit(solution)/shard_map/all_gather | solution.py:27
  63.6 3.8 fusion.2
  67.7 2.0 multiply_convert_fusion.4
  69.7 1231.7 %while.20 = (s32[]{:T(128)}, f32[192,128]{1,0:T(8,128)S(1)}, f32[192,128]{1,0:T(8,128)}, bf16[192,4096]{1,0:T(8,128)(2,1)S(1)}, pred[]{:T(512)}, /*index=5*/f32[...) while((s32[]{:T(128)}, f32[192,128]{1,0:T(8,128)S(1)}, ...), condition=%wide.region_4.5_spmd.clone, body=%wide.region_0.4_spmd.clone.sunk | while | flops 2117640192 | bytes 78512592 | solution.py:74
  70.5 50.9 %all-gather.6.cloned.1.call-done = bf16[192,4096]{1,0:T(8,128)(2,1)} async-done(((bf16[192,128]{1,0:T(8,128)(2,1)}), bf16[192,4096]{1,0:T(8,128)(2,1)}) %all-gather.6.cloned.1.call-update) | async-done | bytes 1572880 | tf_op jit(solution)/shard_map/while/body/eval_jaxpr/all_gather | solution.py:58
  121.5 2.5 copy.19
  124.1 89.1 %reduce-scatter.6.cloned.1.call-done = bf16[128,192]{1,0:T(8,128)(2,1)} async-done(((bf16[4096,192]{1,0:T(8,128)(2,1)}), bf16[128,192]{1,0:T(8,128)(2,1)}) %reduce-scatter.6.cloned.1.call-update) | async-done | bytes 49168 | tf_op jit(solution)/shard_map/while
  218.2 2.9 collective-permute-done
  222.0 53.7 %all-gather.6.cloned.1.call-done = bf16[192,4096]{1,0:T(8,128)(2,1)} async-done(((bf16[192,128]{1,0:T(8,128)(2,1)}), bf16[192,4096]{1,0:T(8,128)(2,1)}) %all-gather.6.cloned.1.call-update) | async-done | bytes 1572880 | tf_op jit(solution)/shard_map/while/body/eval_jaxpr/all_gather | solution.py:58
  275.8 2.5 copy.19
  278.4 89.9 %reduce-scatter.6.cloned.1.call-done = bf16[128,192]{1,0:T(8,128)(2,1)} async-done(((bf16[4096,192]{1,0:T(8,128)(2,1)}), bf16[128,192]{1,0:T(8,128)(2,1)}) %reduce-scatter.6.cloned.1.call-update) | async-done | bytes 49168 | tf_op jit(solution)/shard_map/while
  369.8 1.6 select_select_fusion.6
  373.3 2.9 collective-permute-done
  377.1 53.7 %all-gather.6.cloned.1.call-done = bf16[192,4096]{1,0:T(8,128)(2,1)} async-done(((bf16[192,128]{1,0:T(8,128)(2,1)}), bf16[192,4096]{1,0:T(8,128)(2,1)}) %all-gather.6.cloned.1.call-update) | async-done | bytes 1572880 | tf_op jit(solution)/shard_map/while/body/eval_jaxpr/all_gather | solution.py:58
  430.9 2.5 copy.19
  433.5 90.7 %reduce-scatter.6.cloned.1.call-done = bf16[128,192]{1,0:T(8,128)(2,1)} async-done(((bf16[4096,192]{1,0:T(8,128)(2,1)}), bf16[128,192]{1,0:T(8,128)(2,1)}) %reduce-scatter.6.cloned.1.call-update) | async-done | bytes 49168 | tf_op jit(solution)/shard_map/while
  529.3 2.9 collective-permute-done
  533.0 54.0 %all-gather.6.cloned.1.call-done = bf16[192,4096]{1,0:T(8,128)(2,1)} async-done(((bf16[192,128]{1,0:T(8,128)(2,1)}), bf16[192,4096]{1,0:T(8,128)(2,1)}) %all-gather.6.cloned.1.call-update) | async-done | bytes 1572880 | tf_op jit(solution)/shard_map/while/body/eval_jaxpr/all_gather | solution.py:58
  587.2 2.5 copy.19
  589.7 91.5 %reduce-scatter.6.cloned.1.call-done = bf16[128,192]{1,0:T(8,128)(2,1)} async-done(((bf16[4096,192]{1,0:T(8,128)(2,1)}), bf16[128,192]{1,0:T(8,128)(2,1)}) %reduce-scatter.6.cloned.1.call-update) | async-done | bytes 49168 | tf_op jit(solution)/shard_map/while
  686.3 2.9 collective-permute-done
  690.1 53.7 %all-gather.6.cloned.1.call-done = bf16[192,4096]{1,0:T(8,128)(2,1)} async-done(((bf16[192,128]{1,0:T(8,128)(2,1)}), bf16[192,4096]{1,0:T(8,128)(2,1)}) %all-gather.6.cloned.1.call-update) | async-done | bytes 1572880 | tf_op jit(solution)/shard_map/while/body/eval_jaxpr/all_gather | solution.py:58
  743.9 2.5 copy.19
  746.5 89.3 %reduce-scatter.6.cloned.1.call-done = bf16[128,192]{1,0:T(8,128)(2,1)} async-done(((bf16[4096,192]{1,0:T(8,128)(2,1)}), bf16[128,192]{1,0:T(8,128)(2,1)}) %reduce-scatter.6.cloned.1.call-update) | async-done | bytes 49168 | tf_op jit(solution)/shard_map/while
  840.9 2.9 collective-permute-done
  844.6 53.7 %all-gather.6.cloned.1.call-done = bf16[192,4096]{1,0:T(8,128)(2,1)} async-done(((bf16[192,128]{1,0:T(8,128)(2,1)}), bf16[192,4096]{1,0:T(8,128)(2,1)}) %all-gather.6.cloned.1.call-update) | async-done | bytes 1572880 | tf_op jit(solution)/shard_map/while/body/eval_jaxpr/all_gather | solution.py:58
  898.5 2.5 copy.19
  901.0 88.3 %reduce-scatter.6.cloned.1.call-done = bf16[128,192]{1,0:T(8,128)(2,1)} async-done(((bf16[4096,192]{1,0:T(8,128)(2,1)}), bf16[128,192]{1,0:T(8,128)(2,1)}) %reduce-scatter.6.cloned.1.call-update) | async-done | bytes 49168 | tf_op jit(solution)/shard_map/while
  994.4 2.9 collective-permute-done
  998.2 53.7 %all-gather.6.cloned.1.call-done = bf16[192,4096]{1,0:T(8,128)(2,1)} async-done(((bf16[192,128]{1,0:T(8,128)(2,1)}), bf16[192,4096]{1,0:T(8,128)(2,1)}) %all-gather.6.cloned.1.call-update) | async-done | bytes 1572880 | tf_op jit(solution)/shard_map/while/body/eval_jaxpr/all_gather | solution.py:58
  1052.0 2.5 copy.19
  1054.5 87.3 %reduce-scatter.6.cloned.1.call-done = bf16[128,192]{1,0:T(8,128)(2,1)} async-done(((bf16[4096,192]{1,0:T(8,128)(2,1)}), bf16[128,192]{1,0:T(8,128)(2,1)}) %reduce-scatter.6.cloned.1.call-update) | async-done | bytes 49168 | tf_op jit(solution)/shard_map/while
  1146.9 2.9 collective-permute-done
  1150.7 53.7 %all-gather.6.cloned.1.call-done = bf16[192,4096]{1,0:T(8,128)(2,1)} async-done(((bf16[192,128]{1,0:T(8,128)(2,1)}), bf16[192,4096]{1,0:T(8,128)(2,1)}) %all-gather.6.cloned.1.call-update) | async-done | bytes 1572880 | tf_op jit(solution)/shard_map/while/body/eval_jaxpr/all_gather | solution.py:58
  1204.4 7.6 conditional.3
  1204.4 3.8 fusion.18
  1212.0 2.5 copy.19
  1214.6 78.9 %reduce-scatter.6.cloned.1.call-done = bf16[128,192]{1,0:T(8,128)(2,1)} async-done(((bf16[4096,192]{1,0:T(8,128)(2,1)}), bf16[128,192]{1,0:T(8,128)(2,1)}) %reduce-scatter.6.cloned.1.call-update) | async-done | bytes 49168 | tf_op jit(solution)/shard_map/while
  1298.5 2.9 collective-permute-done
  1301.4 2.0 fusion.9
  1305.5 5.8 sqrt_multiply_fusion
  1311.4 9.4 reshape.25
  1320.8 4.8 iota.3
  1325.6 80.7 %sort.15 = (f32[112,4,4096]{2,1,0:T(4,128)}, s32[112,4,4096]{2,1,0:T(4,128)}) sort(f32[112,4,4096]{2,1,0:T(4,128)} %reshape.25, s32[112,4,4096]{2,1,0:T(4,128)} %iota.3), dimensions={1}, to_apply=%region_5.6 | sort | flops 38535168 | bytes 29360128 | tf_op jit(solution)/shard_map/jit(sort)/sort | solution.py:84
  1406.4 9.0 add_bitcast_fusion
  1415.4 2.6 copy.14
  (131 shorter events, 54.4 us)
Async XLA Ops:
  7.2 56.4 %all-gather.4.cloned.1.call-start = ((), (), s32[]{:S(2)}) async-start(), calls=%async_computation.1 | async-start | bytes 1622016 | tf_op jit(solution)/shard_map/all_gather | solution.py:27
  63.6 3.9 copy-start.5
  63.6 4.1 copy-start.7
  69.7 51.7 %all-gather.6.cloned.1.call-start = ((), (), s32[]{:S(2)}) async-start(), calls=%async_computation.2 | async-start | bytes 1622016 | tf_op jit(solution)/shard_map/while/body/eval_jaxpr/all_gather | solution.py:58
  70.4 142.7 %reduce-scatter.6.cloned.1.call-start = ((), (), s32[]{:S(2)}) async-start(), calls=%async_computation.3 | async-start | bytes 2162688 | tf_op jit(solution)/shard_map/while
  124.1 93.5 %copy-start.2 = (bf16[192,4096]{1,0:T(8,128)(2,1)S(1)}, bf16[192,4096]{1,0:T(8,128)(2,1)}, u32[]{:S(2)}) copy-start(bf16[192,4096]{1,0:T(8,128)(2,1)} %all-gather.6.cloned.1.call-done) | copy-start | bytes 4718596 | tf_op jit(solution)/shard_map/while
  216.3 4.8 collective-permute-start
  221.1 54.5 %all-gather.6.cloned.1.call-start = ((), (), s32[]{:S(2)}) async-start(), calls=%async_computation.2 | async-start | bytes 1622016 | tf_op jit(solution)/shard_map/while/body/eval_jaxpr/all_gather | solution.py:58
  221.9 146.3 %reduce-scatter.6.cloned.1.call-start = ((), (), s32[]{:S(2)}) async-start(), calls=%async_computation.3 | async-start | bytes 2162688 | tf_op jit(solution)/shard_map/while
  278.3 94.4 %copy-start.2 = (bf16[192,4096]{1,0:T(8,128)(2,1)S(1)}, bf16[192,4096]{1,0:T(8,128)(2,1)}, u32[]{:S(2)}) copy-start(bf16[192,4096]{1,0:T(8,128)(2,1)} %all-gather.6.cloned.1.call-done) | copy-start | bytes 4718596 | tf_op jit(solution)/shard_map/while
  371.4 4.8 collective-permute-start
  376.2 54.5 %all-gather.6.cloned.1.call-start = ((), (), s32[]{:S(2)}) async-start(), calls=%async_computation.2 | async-start | bytes 1622016 | tf_op jit(solution)/shard_map/while/body/eval_jaxpr/all_gather | solution.py:58
  377.0 147.2 %reduce-scatter.6.cloned.1.call-start = ((), (), s32[]{:S(2)}) async-start(), calls=%async_computation.3 | async-start | bytes 2162688 | tf_op jit(solution)/shard_map/while
  433.4 95.2 %copy-start.2 = (bf16[192,4096]{1,0:T(8,128)(2,1)S(1)}, bf16[192,4096]{1,0:T(8,128)(2,1)}, u32[]{:S(2)}) copy-start(bf16[192,4096]{1,0:T(8,128)(2,1)} %all-gather.6.cloned.1.call-done) | copy-start | bytes 4718596 | tf_op jit(solution)/shard_map/while
  527.3 4.8 collective-permute-start
  532.2 54.8 %all-gather.6.cloned.1.call-start = ((), (), s32[]{:S(2)}) async-start(), calls=%async_computation.2 | async-start | bytes 1622016 | tf_op jit(solution)/shard_map/while/body/eval_jaxpr/all_gather | solution.py:58
  533.0 148.3 %reduce-scatter.6.cloned.1.call-start = ((), (), s32[]{:S(2)}) async-start(), calls=%async_computation.3 | async-start | bytes 2162688 | tf_op jit(solution)/shard_map/while
  589.7 96.0 %copy-start.2 = (bf16[192,4096]{1,0:T(8,128)(2,1)S(1)}, bf16[192,4096]{1,0:T(8,128)(2,1)}, u32[]{:S(2)}) copy-start(bf16[192,4096]{1,0:T(8,128)(2,1)} %all-gather.6.cloned.1.call-done) | copy-start | bytes 4718596 | tf_op jit(solution)/shard_map/while
  684.4 4.8 collective-permute-start
  689.2 54.5 %all-gather.6.cloned.1.call-start = ((), (), s32[]{:S(2)}) async-start(), calls=%async_computation.2 | async-start | bytes 1622016 | tf_op jit(solution)/shard_map/while/body/eval_jaxpr/all_gather | solution.py:58
  690.0 145.8 %reduce-scatter.6.cloned.1.call-start = ((), (), s32[]{:S(2)}) async-start(), calls=%async_computation.3 | async-start | bytes 2162688 | tf_op jit(solution)/shard_map/while
  746.4 93.8 %copy-start.2 = (bf16[192,4096]{1,0:T(8,128)(2,1)S(1)}, bf16[192,4096]{1,0:T(8,128)(2,1)}, u32[]{:S(2)}) copy-start(bf16[192,4096]{1,0:T(8,128)(2,1)} %all-gather.6.cloned.1.call-done) | copy-start | bytes 4718596 | tf_op jit(solution)/shard_map/while
  838.9 4.8 collective-permute-start
  843.8 54.5 %all-gather.6.cloned.1.call-start = ((), (), s32[]{:S(2)}) async-start(), calls=%async_computation.2 | async-start | bytes 1622016 | tf_op jit(solution)/shard_map/while/body/eval_jaxpr/all_gather | solution.py:58
  844.6 144.7 %reduce-scatter.6.cloned.1.call-start = ((), (), s32[]{:S(2)}) async-start(), calls=%async_computation.3 | async-start | bytes 2162688 | tf_op jit(solution)/shard_map/while
  901.0 92.8 %copy-start.2 = (bf16[192,4096]{1,0:T(8,128)(2,1)S(1)}, bf16[192,4096]{1,0:T(8,128)(2,1)}, u32[]{:S(2)}) copy-start(bf16[192,4096]{1,0:T(8,128)(2,1)} %all-gather.6.cloned.1.call-done) | copy-start | bytes 4718596 | tf_op jit(solution)/shard_map/while
  992.5 4.8 collective-permute-start
  997.3 54.5 %all-gather.6.cloned.1.call-start = ((), (), s32[]{:S(2)}) async-start(), calls=%async_computation.2 | async-start | bytes 1622016 | tf_op jit(solution)/shard_map/while/body/eval_jaxpr/all_gather | solution.py:58
  998.1 143.8 %reduce-scatter.6.cloned.1.call-start = ((), (), s32[]{:S(2)}) async-start(), calls=%async_computation.3 | async-start | bytes 2162688 | tf_op jit(solution)/shard_map/while
  1054.5 91.8 %copy-start.2 = (bf16[192,4096]{1,0:T(8,128)(2,1)S(1)}, bf16[192,4096]{1,0:T(8,128)(2,1)}, u32[]{:S(2)}) copy-start(bf16[192,4096]{1,0:T(8,128)(2,1)} %all-gather.6.cloned.1.call-done) | copy-start | bytes 4718596 | tf_op jit(solution)/shard_map/while
  1145.0 4.8 collective-permute-start
  1149.9 54.5 %all-gather.6.cloned.1.call-start = ((), (), s32[]{:S(2)}) async-start(), calls=%async_computation.2 | async-start | bytes 1622016 | tf_op jit(solution)/shard_map/while/body/eval_jaxpr/all_gather | solution.py:58
  1150.6 142.8 %reduce-scatter.6.cloned.1.call-start = ((), (), s32[]{:S(2)}) async-start(), calls=%async_computation.3 | async-start | bytes 2162688 | tf_op jit(solution)/shard_map/while
  1204.4 3.9 copy-start.1
  1208.2 2.2 copy-start
  1208.2 2.2 copy-start.3
  1214.5 83.3 %copy-start.2 = (bf16[192,4096]{1,0:T(8,128)(2,1)S(1)}, bf16[192,4096]{1,0:T(8,128)(2,1)}, u32[]{:S(2)}) copy-start(bf16[192,4096]{1,0:T(8,128)(2,1)} %all-gather.6.cloned.1.call-done) | copy-start | bytes 4718596 | tf_op jit(solution)/shard_map/while
  1296.6 4.8 collective-permute-start
  1301.4 2.1 copy-start.6
  1303.5 2.0 copy-start.4
Sparse Core Ops, SparseCore 0:
  10.5 53.0 all-gather.3
  73.0 48.3 all-gather.5
  125.2 87.9 reduce-scatter.5
  224.1 51.4 all-gather.5
  279.3 88.8 reduce-scatter.5
  379.2 51.4 all-gather.5
  434.6 89.5 reduce-scatter.5
  535.5 51.4 all-gather.5
  590.8 90.3 reduce-scatter.5
  692.2 51.4 all-gather.5
  747.6 88.1 reduce-scatter.5
  846.8 51.4 all-gather.5
  902.1 87.1 reduce-scatter.5
  1000.3 51.4 all-gather.5
  1055.5 86.3 reduce-scatter.5
  1152.9 51.4 all-gather.5
  1214.7 78.6 reduce-scatter.5
where the time goes:
time: 1430 us; the launch traced here: 1420 us
  waiting for transfers between devices  1200 us (84%)
  other arithmetic  113 us (8%)
  local copies, waits for them, and re-layouts  65.3 us (5%)
  matrix products  21.8 us (2%)
    while x24, waiting for transfers between devices  705 us
    all_gather x8, waiting for transfers between devices, advance(): lax.all_gather(grad_in.astype(jnp.bfloat16), 'tp', axis=1, tiled=True)  427 us
    sort x1, other arithmetic, shards(): ordered = jnp.sort(score.reshape(hidden_cols // 4, 4, model_width), axis=1)  80.7 us
    all_gather x1, waiting for transfers between devices, shards(): piece = lax.all_gather(local_inputs, 'tp', axis=1, tiled=True)  42.7 us
    while x32, local copies, waits for them, and re-layouts  32.6 us
  transfers between devices with their start and end apart: 25, of which 25 were waited for; matrix products, arithmetic and copies ran while one was open for 1% of the time, Pallas kernels for 0%

commit v1 on v0

v1 whole, which is shorter than its diff:
```python
import functools

import jax
import jax.numpy as jnp
from jax import lax
from jax.experimental import pallas as pl
from jax.experimental.pallas import tpu as pltpu
from jax.sharding import PartitionSpec as P

SAMPLES = 3
CHUNK = 128
ROWS_PER_STEP = 32
MESH = pl.DeviceIdType.MESH
BF16 = jnp.bfloat16
F32 = jnp.float32


def grid_sides(chips):
    side = 1
    while side * side < chips:
        side *= 2
    return chips // side, side


def ring_distance(step, size):
    return min(step, size - step)


def chip_offsets(nx, ny):
    offsets = [(dx, dy) for dx in range(nx) for dy in range(ny)]
    return sorted(offsets, key=lambda o: -(ring_distance(o[0], nx) + ring_distance(o[1], ny)))


def kernel(
    sections,
    chips,
    rows,
    step_rows,
    units,
    x_ref,
    top_ref,
    wg_hbm,
    wu_hbm,
    wd_hbm,
    grad_ref,
    kept_ref,
    w_gate,
    w_up,
    w_down,
    w_own,
    down_t,
    both_t,
    x_all,
    g_all,
    g_other,
    top16,
    result16,
    send_buf,
    recv_buf,
    part_mine,
    part_other,
    pre_mine,
    pre_other,
    factor_gate,
    factor_up,
    hidden_t,
    load_sem,
    swap_sem,
    x_sem,
    pre_sem,
    gather_sem,
    below_sem,
    part_sem,
    forward_sem,
    term_sem,
):
    nx, ny = grid_sides(chips)
    offsets = chip_offsets(nx, ny)
    steps = rows // step_rows
    half = chips * CHUNK
    section = lax.axis_index("section")
    index = lax.axis_index("tp")
    chip, core = index // 2, lax.rem(index, 2)
    other = 1 - core
    chip_x, chip_y = chip // ny, lax.rem(chip, ny)
    places = [lax.rem(chip_x + dx, nx) * ny + lax.rem(chip_y + dy, ny) for dx, dy in offsets]
    sibling = (section, 2 * chip + other)
    above = lax.rem(section + 1, sections)
    below = lax.rem(section + sections - 1, sections)
    is_top = section == sections - 1
    is_last = section == 0

    pltpu.make_async_copy(wg_hbm.at[:, core], w_gate.at[core], load_sem.at[0]).start()
    pltpu.make_async_copy(wu_hbm.at[:, core], w_up.at[core], load_sem.at[1]).start()
    for k in range(chips):
        mine = pl.ds(pl.multiple_of((2 * k + core) * CHUNK, CHUNK), CHUNK)
        pltpu.make_async_copy(
            wd_hbm.at[:, mine], w_down.at[core, :, pl.ds(k * CHUNK, CHUNK)], load_sem.at[2]
        ).start()
    pltpu.make_async_copy(wd_hbm, w_own, load_sem.at[3]).start()

    barrier = pltpu.get_barrier_semaphore()
    pl.semaphore_signal(barrier, inc=1, device_id=sibling, device_id_type=MESH)
    for place in places[:-1]:
        pl.semaphore_signal(
            barrier, inc=1, device_id=(section, 2 * place + core), device_id_type=MESH
        )

    @pl.when(jnp.logical_not(is_top))
    def _():
        for place in places:
            pl.semaphore_signal(
                barrier, inc=1, device_id=(above, 2 * place + core), device_id_type=MESH
            )

    @pl.when(jnp.logical_not(is_last))
    def _():
        for place in places:
            pl.semaphore_signal(
                barrier, inc=1, device_id=(below, 2 * place + core), device_id_type=MESH
            )

    top16[...] = top_ref[...].astype(BF16)
    neighbours = (
        chips
        + jnp.where(is_top, 0, chips)
        + jnp.where(is_last, 0, chips)
    )
    pl.semaphore_wait(barrier, neighbours)

    def spread_top(step):
        at = pl.ds(step * step_rows, step_rows)
        for place in places[:-1]:
            pltpu.make_async_remote_copy(
                src_ref=top16.at[at],
                dst_ref=g_all.at[chip, at],
                send_sem=below_sem.at[steps + step],
                recv_sem=gather_sem.at[step],
                device_id=(section, 2 * place + core),
                device_id_type=MESH,
            ).start()
        pltpu.make_async_copy(top16.at[at], g_all.at[chip, at], gather_sem.at[step]).start()

    @pl.when(is_top)
    def _():
        spread_top(0)

    for n, (source, target) in enumerate(((wg_hbm, w_gate), (wu_hbm, w_up))):
        pltpu.make_async_remote_copy(
            src_ref=source.at[:, other],
            dst_ref=target.at[core],
            send_sem=swap_sem.at[n],
            recv_sem=swap_sem.at[3 + n],
            device_id=sibling,
            device_id_type=MESH,
        ).start()
    for place in places[:-1]:
        pltpu.make_async_remote_copy(
            src_ref=x_ref,
            dst_ref=x_all.at[chip],
            send_sem=x_sem.at[0],
            recv_sem=x_sem.at[1],
            device_id=(section, 2 * place + core),
            device_id_type=MESH,
        ).start()
    pltpu.make_async_copy(x_ref, x_all.at[chip], x_sem.at[1]).start()
    for k in range(chips):
        theirs = pl.ds(pl.multiple_of((2 * k + other) * CHUNK, CHUNK), CHUNK)
        pltpu.make_async_remote_copy(
            src_ref=wd_hbm.at[:, theirs],
            dst_ref=w_down.at[core, :, pl.ds(k * CHUNK, CHUNK)],
            send_sem=swap_sem.at[2],
            recv_sem=swap_sem.at[5],
            device_id=sibling,
            device_id_type=MESH,
        ).start()

    @pl.when(is_top)
    def _():
        for step in range(1, steps):
            spread_top(step)

    def wait(ref, sem):
        pltpu.make_async_copy(ref, ref, sem).wait()

    wait(w_gate.at[core], load_sem.at[0])
    wait(w_up.at[core], load_sem.at[1])
    wait(x_all, x_sem.at[1])
    wait(w_gate.at[other], swap_sem.at[3])
    wait(w_up.at[other], swap_sem.at[4])
    x_rows = jnp.concatenate([x_all[k] for k in range(chips)], axis=1)
    for n, weight in enumerate((w_gate, w_up)):
        for h in range(2):
            pre_mine[n, h] = jnp.dot(
                x_rows, weight[h].reshape(half, units), preferred_element_type=F32
            )
        pltpu.make_async_remote_copy(
            src_ref=pre_mine.at[n],
            dst_ref=pre_other.at[n],
            send_sem=pre_sem.at[n],
            recv_sem=pre_sem.at[2 + n],
            device_id=sibling,
            device_id_type=MESH,
        ).start()

    for n, weight in enumerate((w_gate, w_up)):
        for h in range(2):
            for t, place in enumerate(places):
                both_t[pl.ds((2 * n + h) * units, units), pl.ds(t * CHUNK, CHUNK)] = weight[h, place].T
    wait(w_down.at[core], load_sem.at[2])
    wait(w_down.at[other], swap_sem.at[5])
    for k in range(chips):
        at = pl.ds(k * CHUNK, CHUNK)
        down_t[at, :] = jnp.concatenate([w_down[0, :, at], w_down[1, :, at]], axis=0).T

    fourth = units // 4
    to_place = lax.broadcasted_iota(jnp.int32, (units, units), 0)
    from_unit = lax.broadcasted_iota(jnp.int32, (units, units), 1)
    member = (
        (to_place >= fourth).astype(jnp.int32)
        + (to_place >= 2 * fourth).astype(jnp.int32)
        + (to_place >= 3 * fourth).astype(jnp.int32)
    )
    spread = (from_unit == 4 * (to_place - member * fourth) + member).astype(F32).astype(BF16)

    wait(pre_other.at[0], pre_sem.at[2])
    wait(pre_other.at[1], pre_sem.at[3])
    gates, ups = [], []
    for h in range(2):
        pre_gate = pre_mine[0, h] + pre_other[0, h]
        pre_up = pre_mine[1, h] + pre_other[1, h]
        sigmoid = jax.nn.sigmoid(pre_gate)
        silu = pre_gate * sigmoid
        gates.append(pre_up * (sigmoid * (1.0 + pre_gate * (1.0 - sigmoid))))
        ups.append(silu)
        hidden = (silu * pre_up).astype(BF16)

        @pl.when(core == h)
        def _():
            for sample in range(SAMPLES):
                some = hidden[sample * (rows // SAMPLES) : (sample + 1) * (rows // SAMPLES)]
                hidden_t[sample] = lax.dot_general(
                    spread, some, (((1,), (1,)), ((), ())), preferred_element_type=F32
                ).astype(BF16)

    factor_gate[...] = jnp.concatenate(gates, axis=1)
    factor_up[...] = jnp.concatenate(ups, axis=1)

    def rows_of(step):
        return pl.ds(pl.multiple_of(step * step_rows, step_rows), step_rows)

    def first(step):
        at = rows_of(step)
        wait(g_all.at[:, at], gather_sem.at[step])
        grads = jnp.concatenate([g_all[k, at, :] for k in range(chips)], axis=1)
        part_mine[at, :] = jnp.dot(grads, down_t[...], preferred_element_type=F32)
        pltpu.make_async_remote_copy(
            src_ref=part_mine.at[at],
            dst_ref=part_other.at[at],
            send_sem=part_sem.at[0, step],
            recv_sem=part_sem.at[1, step],
            device_id=sibling,
            device_id_type=MESH,
        ).start()
        pltpu.make_async_remote_copy(
            src_ref=g_all.at[:, at],
            dst_ref=g_other.at[:, at],
            send_sem=forward_sem.at[0, step],
            recv_sem=forward_sem.at[1, step],
            device_id=sibling,
            device_id_type=MESH,
        ).start()

    def second(step):
        at = rows_of(step)
        wait(part_other.at[at], part_sem.at[1, step])
        hidden_grad = part_mine[at, :] + part_other[at, :]
        both = jnp.concatenate(
            [
                (hidden_grad * factor_gate[at, :]).astype(BF16),
                (hidden_grad * factor_up[at, :]).astype(BF16),
            ],
            axis=1,
        )
        for pair in range(chips // 2):
            term = jnp.dot(
                both,
                both_t[:, pl.ds(2 * pair * CHUNK, 2 * CHUNK)],
                preferred_element_type=F32,
            ).astype(BF16)
            for t in (2 * pair, 2 * pair + 1):
                send_buf[t, at, :] = term[:, (t - 2 * pair) * CHUNK : (t - 2 * pair + 1) * CHUNK]
                if t < chips - 1:
                    pltpu.make_async_remote_copy(
                        src_ref=send_buf.at[t, at],
                        dst_ref=recv_buf.at[t, at],
                        send_sem=term_sem.at[0, step],
                        recv_sem=term_sem.at[1, step],
                        device_id=(section, 2 * places[t] + core),
                        device_id_type=MESH,
                    ).start()

    def third(step):
        at = rows_of(step)
        wait(recv_buf.at[:, at], term_sem.at[1, step])
        total = send_buf[chips - 1, at, :].astype(F32)
        for t in range(chips - 1):
            total = total + recv_buf[t, at, :].astype(F32)
        result = jnp.where(is_top, top_ref[at, :], g_all[chip, at, :].astype(F32)) + total
        grad_ref[at, :] = result
        result16[at, :] = result.astype(BF16)

        @pl.when(jnp.logical_not(is_last))
        def _():
            for place in places:
                pltpu.make_async_remote_copy(
                    src_ref=result16.at[at],
                    dst_ref=g_all.at[chip, at],
                    send_sem=below_sem.at[step],
                    recv_sem=gather_sem.at[step],
                    device_id=(below, 2 * place + core),
                    device_id_type=MESH,
                ).start()

    lag = 2

    @pl.loop(0, steps)
    def _(step):
        first(step)

        @pl.when(step >= lag)
        def _():
            third(step - lag)

        second(step)

    @pl.loop(steps - lag, steps)
    def _(step):
        third(step)

    wait(w_own, load_sem.at[3])

    @pl.loop(0, steps)
    def _(step):
        wait(g_other.at[:, rows_of(step)], forward_sem.at[1, step])

    per_sample = rows // SAMPLES

    @pl.loop(0, chips // 2)
    def _(pair):
        for grads, parity in ((g_all, core), (g_other, other)):
            blocks = [2 * pair, 2 * pair + 1]
            columns = [pl.ds(pl.multiple_of((2 * k + parity) * CHUNK, CHUNK), CHUNK) for k in blocks]
            squares = None
            for sample in range(SAMPLES):
                some = jnp.concatenate(
                    [grads[k, pl.ds(sample * per_sample, per_sample), :] for k in blocks], axis=1
                )
                weight_grad = jnp.dot(hidden_t[sample], some, preferred_element_type=F32)
                square = weight_grad * weight_grad
                squares = square if squares is None else squares + square
            weight = jnp.dot(
                spread,
                jnp.concatenate([w_own[:, c] for c in columns], axis=1),
                preferred_element_type=F32,
            )
            score = jnp.abs(weight) * jnp.sqrt(squares)
            a, b, c, d = [score[i * fourth : (i + 1) * fourth] for i in range(4)]
            high_ab, low_ab = jnp.maximum(a, b), jnp.minimum(a, b)
            high_cd, low_cd = jnp.maximum(c, d), jnp.minimum(c, d)
            best = jnp.maximum(high_ab, high_cd)
            next_best = jnp.maximum(jnp.minimum(high_ab, high_cd), jnp.maximum(low_ab, low_cd))
            kept = best + next_best
            for n in range(2):
                kept_ref[:, columns[n]] = kept[:, n * CHUNK : (n + 1) * CHUNK]

    wait(w_gate.at[core], swap_sem.at[0])
    wait(w_up.at[core], swap_sem.at[1])
    wait(w_down.at[core], swap_sem.at[2])
    wait(x_all.at[pl.ds(0, chips - 1)], x_sem.at[0])
    wait(pre_mine.at[0], pre_sem.at[0])
    wait(pre_mine.at[1], pre_sem.at[1])

    @pl.loop(0, steps)
    def _(step):
        at = rows_of(step)
        wait(part_mine.at[at], part_sem.at[0, step])
        wait(g_all.at[:, at], forward_sem.at[0, step])
        wait(recv_buf.at[:, at], term_sem.at[0, step])

        @pl.when(jnp.logical_not(is_last))
        def _():
            wait(g_all.at[:, at], below_sem.at[step])

        @pl.when(is_top)
        def _():
            wait(recv_buf.at[:, at], below_sem.at[steps + step])


def shards(sections, section_inputs, top_gradient, gate_weight, up_weight, down_weight):
    _, rows, width = section_inputs.shape
    _, model, units = gate_weight.shape
    chips = model // CHUNK // 2
    step_rows = ROWS_PER_STEP
    steps = rows // step_rows
    half = chips * CHUNK
    vmem = pl.BlockSpec(memory_space=pltpu.VMEM)
    hbm = pl.BlockSpec(memory_space=pl.ANY)
    dma = pltpu.SemaphoreType.DMA
    grads, kept = pl.pallas_call(
        functools.partial(kernel, sections, chips, rows, step_rows, units),
        out_shape=(
            jax.ShapeDtypeStruct((rows, width), F32),
            jax.ShapeDtypeStruct((units // 4, model), F32),
        ),
        in_specs=[vmem, vmem, hbm, hbm, hbm],
        out_specs=(vmem, vmem),
        scratch_shapes=[
            pltpu.VMEM((2, chips, CHUNK, units), BF16),
            pltpu.VMEM((2, chips, CHUNK, units), BF16),
            pltpu.VMEM((2, units, half), BF16),
            pltpu.VMEM((units, model), BF16),
            pltpu.VMEM((half, 2 * units), BF16),
            pltpu.VMEM((4 * units, half), BF16),
            pltpu.VMEM((chips, rows, CHUNK), BF16),
            pltpu.VMEM((chips, rows, CHUNK), BF16),
            pltpu.VMEM((chips, rows, CHUNK), BF16),
            pltpu.VMEM((rows, CHUNK), BF16),
            pltpu.VMEM((rows, CHUNK), BF16),
            pltpu.VMEM((chips, rows, CHUNK), BF16),
            pltpu.VMEM((chips - 1, rows, CHUNK), BF16),
            pltpu.VMEM((rows, 2 * units), F32),
            pltpu.VMEM((rows, 2 * units), F32),
            pltpu.VMEM((2, 2, rows, units), F32),
            pltpu.VMEM((2, 2, rows, units), F32),
            pltpu.VMEM((rows, 2 * units), F32),
            pltpu.VMEM((rows, 2 * units), F32),
            pltpu.VMEM((SAMPLES, units, rows // SAMPLES), BF16),
            dma((4,)),
            dma((6,)),
            dma((2,)),
            dma((4,)),
            dma((steps,)),
            dma((2 * steps,)),
            dma((2, steps)),
            dma((2, steps)),
            dma((2, steps)),
        ],
        compiler_params=pltpu.CompilerParams(
            collective_id=0, has_side_effects=True, vmem_limit_bytes=56 * 1024 * 1024
        ),
    )(
        section_inputs[0],
        top_gradient,
        gate_weight[0].reshape(chips, 2, CHUNK, units),
        up_weight[0].reshape(chips, 2, CHUNK, units),
        down_weight[0],
    )
    return (grads[None], kept[None])


def solution(mesh):
    in_specs = (
        P("section", None, "tp"),
        P(None, "tp"),
        P("section", None, "tp"),
        P("section", None, "tp"),
        P("section", "tp", None),
    )
    out_specs = (P("section", None, "tp"), P("section", "tp", None))
    body = functools.partial(shards, mesh.shape["section"])
    return jax.shard_map(body, mesh=mesh, in_specs=in_specs, out_specs=out_specs, check_vma=False)
```

time: 1430 us -> 204 us (0.14)
  waiting for transfers between devices: 1200 us -> 0 us
  Pallas kernels: 0 us -> 186 us
  other arithmetic: 113 us -> 0 us
  local copies, waits for them, and re-layouts: 65.3 us -> 17.3 us
  matrix products: 21.8 us -> 0 us
    while x24 -> x0, waiting for transfers between devices: 705 us -> none
    all_gather x9 -> x0, waiting for transfers between devices: 470 us -> none  [the longest x8 427 us: advance(): lax.all_gather(grad_in.astype(jnp.bfloat16), 'tp', axis=1, tiled=True)]
    pallas_call x0 -> x1, Pallas kernels: none -> 186 us  [shards(): pl.pallas_call(functools.partial(kernel, sections, chips, rows, step_rows...]
    sort x1 -> x0, other arithmetic: 80.7 us -> none  [shards(): ordered = jnp.sort(score.reshape(hidden_cols // 4, 4, model_width), axis=1)]
    while x32 -> x0, local copies, waits for them, and re-layouts: 32.6 us -> none
    ppermute x8 -> x0, waiting for transfers between devices: 23.3 us -> none  [from_behind(): lax.ppermute(value, axis, [(source, source + steps) for source in range(f...]
    dot_general x8 -> x0, matrix products: 21.8 us -> none  [the longest x3 9.01 us: shards(): lax.dot_general(hidden_rows, grad_rows, (((0,), (0,)), ((), ())), preferr...]
    select_n x16 -> x0, other arithmetic: 17.6 us -> none  [the longest x8 12.8 us: advance(): section_grad = jnp.where(active, result, section_grad)]
  transfers between devices with their start and end apart: 25 -> 0, of which waited for: 25 -> 0; matrix products, arithmetic and copies ran while one was open for 1% -> 0% of each run, Pallas kernels for 0% -> 0%
where the time goes in v1:
time: 204 us; the launch traced here: 203 us
  Pallas kernels  186 us (91%)
  local copies, waits for them, and re-layouts  17.3 us (8%)
    pallas_call x1, Pallas kernels, shards(): pl.pallas_call(functools.partial(kernel, sections, chips, rows, step_rows...  186 us
    unnamed x4, local copies, waits for them, and re-layouts  17.3 us

profile of v1, /device:TPU:1, one launch (start us, length us, event | category | flops | bytes accessed | tf_op | source)
XLA Modules:
  0.0 203.5 jit_solution(17358026580434915446)
XLA Ops:
  0.6 6.4 %copy.7 = bf16[1,4096,448]{2,1,0:T(8,128)(2,1)} copy(bf16[1,4096,448]{1,2,0:T(8,128)(2,1)} %param.7) | data formatting | bytes 7340032 | tf_op args[2]
  7.0 6.5 %copy.8 = bf16[1,4096,448]{2,1,0:T(8,128)(2,1)} copy(bf16[1,4096,448]{1,2,0:T(8,128)(2,1)} %param.8) | data formatting | bytes 7340032 | tf_op args[3]
  13.5 185.5 %shard_map.68 = (f32[192,128]{1,0:T(8,128)}, f32[112,4096]{1,0:T(8,128)}) custom-call(bf16[192,128]{1,0:T(8,128)(2,1)} %bitcast.11, f32[192,128]{1,0:T(8,128)} %top_ref.1, bf16[16,2,128,448]{3,2,1,0:T(8,128)(2,1)} %bitcast.6, bf16[16,2,128,448]{3,2,1,0:T(8,128)(2,1)} %bitcast.7, bf16[448,4096]{1,0:T(8,128)(2,1)} %bitcast.8), custom_call_target="tpu_custom_call" | custom-call | tf_op jit(solution)/shard_map/pallas_call | solution.py:410
  199.0 1.5 copy.11
  200.6 2.9 %copy.12 = f32[1,112,4096]{2,1,0:T(8,128)} copy(f32[1,112,4096]{2,1,0:T(8,128)} %bitcast.9) | data formatting | bytes 3670016

commit v2 on v1

--- a/solution.py
+++ b/solution.py
@@ -44,8 +44,6 @@
     wd_hbm,
     grad_ref,
     kept_ref,
-    w_gate,
-    w_up,
     w_down,
     w_own,
     down_t,
@@ -90,12 +88,21 @@
     is_top = section == sections - 1
     is_last = section == 0
 
-    pltpu.make_async_copy(wg_hbm.at[:, core], w_gate.at[core], load_sem.at[0]).start()
-    pltpu.make_async_copy(wu_hbm.at[:, core], w_up.at[core], load_sem.at[1]).start()
+    def columns_of(place, parity):
+        return pl.ds(pl.multiple_of((2 * place + parity) * CHUNK, CHUNK), CHUNK)
+
+    for n, source in enumerate((wg_hbm, wu_hbm)):
+        for t, place in enumerate(places):
+            pltpu.make_async_copy(
+                source.at[:, columns_of(place, core)],
+                both_t.at[n, core, :, pl.ds(t * CHUNK, CHUNK)],
+                load_sem.at[n],
+            ).start()
     for k in range(chips):
-        mine = pl.ds(pl.multiple_of((2 * k + core) * CHUNK, CHUNK), CHUNK)
         pltpu.make_async_copy(
-            wd_hbm.at[:, mine], w_down.at[core, :, pl.ds(k * CHUNK, CHUNK)], load_sem.at[2]
+            wd_hbm.at[:, columns_of(k, core)],
+            w_down.at[core, :, pl.ds(k * CHUNK, CHUNK)],
+            load_sem.at[2],
         ).start()
     pltpu.make_async_copy(wd_hbm, w_own, load_sem.at[3]).start()
 
@@ -145,15 +152,16 @@
     def _():
         spread_top(0)
 
-    for n, (source, target) in enumerate(((wg_hbm, w_gate), (wu_hbm, w_up))):
-        pltpu.make_async_remote_copy(
-            src_ref=source.at[:, other],
-            dst_ref=target.at[core],
-            send_sem=swap_sem.at[n],
-            recv_sem=swap_sem.at[3 + n],
-            device_id=sibling,
-            device_id_type=MESH,
-        ).start()
+    for n, source in enumerate((wg_hbm, wu_hbm)):
+        for t, place in enumerate(places):
+            pltpu.make_async_remote_copy(
+                src_ref=source.at[:, columns_of(place, other)],
+                dst_ref=both_t.at[n, core, :, pl.ds(t * CHUNK, CHUNK)],
+                send_sem=swap_sem.at[n],
+                recv_sem=swap_sem.at[3 + n],
+                device_id=sibling,
+                device_id_type=MESH,
+            ).start()
     for place in places[:-1]:
         pltpu.make_async_remote_copy(
             src_ref=x_ref,
@@ -165,9 +173,8 @@
         ).start()
     pltpu.make_async_copy(x_ref, x_all.at[chip], x_sem.at[1]).start()
     for k in range(chips):
-        theirs = pl.ds(pl.multiple_of((2 * k + other) * CHUNK, CHUNK), CHUNK)
         pltpu.make_async_remote_copy(
-            src_ref=wd_hbm.at[:, theirs],
+            src_ref=wd_hbm.at[:, columns_of(k, other)],
             dst_ref=w_down.at[core, :, pl.ds(k * CHUNK, CHUNK)],
             send_sem=swap_sem.at[2],
             recv_sem=swap_sem.at[5],
@@ -183,16 +190,14 @@
     def wait(ref, sem):
         pltpu.make_async_copy(ref, ref, sem).wait()
 
-    wait(w_gate.at[core], load_sem.at[0])
-    wait(w_up.at[core], load_sem.at[1])
     wait(x_all, x_sem.at[1])
-    wait(w_gate.at[other], swap_sem.at[3])
-    wait(w_up.at[other], swap_sem.at[4])
-    x_rows = jnp.concatenate([x_all[k] for k in range(chips)], axis=1)
-    for n, weight in enumerate((w_gate, w_up)):
+    x_rows = jnp.concatenate([x_all[place] for place in places], axis=1)
+    for n in range(2):
+        wait(both_t.at[n, core], load_sem.at[n])
+        wait(both_t.at[n, other], swap_sem.at[3 + n])
         for h in range(2):
-            pre_mine[n, h] = jnp.dot(
-                x_rows, weight[h].reshape(half, units), preferred_element_type=F32
+            pre_mine[n, h] = lax.dot_general(
+                x_rows, both_t[n, h], (((1,), (1,)), ((), ())), preferred_element_type=F32
             )
         pltpu.make_async_remote_copy(
             src_ref=pre_mine.at[n],
@@ -203,10 +208,6 @@
             device_id_type=MESH,
         ).start()
 
-    for n, weight in enumerate((w_gate, w_up)):
-        for h in range(2):
-            for t, place in enumerate(places):
-                both_t[pl.ds((2 * n + h) * units, units), pl.ds(t * CHUNK, CHUNK)] = weight[h, place].T
     wait(w_down.at[core], load_sem.at[2])
     wait(w_down.at[other], swap_sem.at[5])
     for k in range(chips):
@@ -285,7 +286,7 @@
         for pair in range(chips // 2):
             term = jnp.dot(
                 both,
-                both_t[:, pl.ds(2 * pair * CHUNK, 2 * CHUNK)],
+                both_t[:, :, :, pl.ds(2 * pair * CHUNK, 2 * CHUNK)].reshape(4 * units, 2 * CHUNK),
                 preferred_element_type=F32,
             ).astype(BF16)
             for t in (2 * pair, 2 * pair + 1):
@@ -334,7 +335,7 @@
 
         second(step)
 
-    @pl.loop(steps - lag, steps)
+    @pl.loop(steps - lag, jnp.where(is_last, steps - lag, steps))
     def _(step):
         third(step)
 
@@ -350,7 +351,7 @@
     def _(pair):
         for grads, parity in ((g_all, core), (g_other, other)):
             blocks = [2 * pair, 2 * pair + 1]
-            columns = [pl.ds(pl.multiple_of((2 * k + parity) * CHUNK, CHUNK), CHUNK) for k in blocks]
+            columns = [columns_of(k, parity) for k in blocks]
             squares = None
             for sample in range(SAMPLES):
                 some = jnp.concatenate(
@@ -374,8 +375,12 @@
             for n in range(2):
                 kept_ref[:, columns[n]] = kept[:, n * CHUNK : (n + 1) * CHUNK]
 
-    wait(w_gate.at[core], swap_sem.at[0])
-    wait(w_up.at[core], swap_sem.at[1])
+    @pl.loop(jnp.where(is_last, steps - lag, steps), steps)
+    def _(step):
+        third(step)
+
+    wait(both_t.at[0, core], swap_sem.at[0])
+    wait(both_t.at[1, core], swap_sem.at[1])
     wait(w_down.at[core], swap_sem.at[2])
     wait(x_all.at[pl.ds(0, chips - 1)], x_sem.at[0])
     wait(pre_mine.at[0], pre_sem.at[0])
@@ -395,6 +400,17 @@
         @pl.when(is_top)
         def _():
             wait(recv_buf.at[:, at], below_sem.at[steps + step])
+
+
+def hand_on(grads_in, kept_in, grads_out, kept_out, sem):
+    copies = [
+        pltpu.make_async_copy(kept_in, kept_out, sem.at[0]),
+        pltpu.make_async_copy(grads_in, grads_out, sem.at[1]),
+    ]
+    for copy in copies:
+        copy.start()
+    for copy in copies:
+        copy.wait()
 
 
 def shards(sections, section_inputs, top_gradient, gate_weight, up_weight, down_weight):
@@ -416,12 +432,10 @@
         in_specs=[vmem, vmem, hbm, hbm, hbm],
         out_specs=(vmem, vmem),
         scratch_shapes=[
-            pltpu.VMEM((2, chips, CHUNK, units), BF16),
-            pltpu.VMEM((2, chips, CHUNK, units), BF16),
             pltpu.VMEM((2, units, half), BF16),
             pltpu.VMEM((units, model), BF16),
             pltpu.VMEM((half, 2 * units), BF16),
-            pltpu.VMEM((4 * units, half), BF16),
+            pltpu.VMEM((2, 2, units, half), BF16),
             pltpu.VMEM((chips, rows, CHUNK), BF16),
             pltpu.VMEM((chips, rows, CHUNK), BF16),
             pltpu.VMEM((chips, rows, CHUNK), BF16),
@@ -452,10 +466,20 @@
     )(
         section_inputs[0],
         top_gradient,
-        gate_weight[0].reshape(chips, 2, CHUNK, units),
-        up_weight[0].reshape(chips, 2, CHUNK, units),
+        gate_weight[0].T,
+        up_weight[0].T,
         down_weight[0],
     )
+    grads, kept = pl.pallas_call(
+        hand_on,
+        out_shape=(
+            jax.ShapeDtypeStruct(grads.shape, F32),
+            jax.ShapeDtypeStruct(kept.shape, F32),
+        ),
+        in_specs=[hbm, hbm],
+        out_specs=(hbm, hbm),
+        scratch_shapes=[dma((2,))],
+    )(grads, kept)
     return (grads[None], kept[None])
 
 

time: 204 us -> 242 us (1.19)
  Pallas kernels: 186 us -> 241 us
  local copies, waits for them, and re-layouts: 17.3 us -> 0 us
    pallas_call x0 -> x1, Pallas kernels: none -> 59.7 us  [shards(): pl.pallas_call(hand_on, out_shape=(jax.ShapeDtypeStruct(grads.shape, F32)...]
    unnamed x4 -> x0, local copies, waits for them, and re-layouts: 17.3 us -> none
    pallas_call x1, Pallas kernels: 186 us -> 182 us  [shards(): pl.pallas_call(functools.partial(kernel, sections, chips, rows, step_rows...]
where the time goes in v2:
time: 242 us
  Pallas kernels  241 us (100%)
    pallas_call x1, Pallas kernels, shards(): pl.pallas_call(functools.partial(kernel, sections, chips, rows, step_rows...  182 us
    pallas_call x1, Pallas kernels, shards(): pl.pallas_call(hand_on, out_shape=(jax.ShapeDtypeStruct(grads.shape, F32)...  59.7 us

profile of v2, /device:TPU:1, one launch (start us, length us, event | category | flops | bytes accessed | tf_op | source)
XLA Modules:
  0.0 242.1 jit_solution(6645498439034493684)
XLA Ops:
  0.6 181.8 %shard_map.68 = (f32[192,128]{1,0:T(8,128)}, f32[112,4096]{1,0:T(8,128)}) custom-call(bf16[192,128]{1,0:T(8,128)(2,1)} %bitcast.13, f32[192,128]{1,0:T(8,128)} %top_ref.1, bf16[448,4096]{1,0:T(8,128)(2,1)} %bitcast.10, bf16[448,4096]{1,0:T(8,128)(2,1)} %bitcast.11, bf16[448,4096]{1,0:T(8,128)(2,1)} %bitcast.12), custom_call_target="tpu_custom_call" | custom-call | tf_op jit(solution)/shard_map/pallas_call | solution.py:426
  182.4 59.7 %shard_map.69 = (f32[192,128]{1,0:T(8,128)}, f32[112,4096]{1,0:T(8,128)}) custom-call(f32[192,128]{1,0:T(8,128)} %get-tuple-element.6.grads_in, f32[112,4096]{1,0:T(8,128)} %get-tuple-element.7.kept_in), custom_call_target="tpu_custom_call" | custom-call | tf_op jit(solution)/shard_map/pallas_call | solution.py:473

commit v3 on v2

--- a/solution.py
+++ b/solution.py
@@ -327,12 +327,11 @@
 
     @pl.loop(0, steps)
     def _(step):
-        first(step)
-
         @pl.when(step >= lag)
         def _():
             third(step - lag)
 
+        first(step)
         second(step)
 
     @pl.loop(steps - lag, jnp.where(is_last, steps - lag, steps))
@@ -402,15 +401,9 @@
             wait(recv_buf.at[:, at], below_sem.at[steps + step])
 
 
-def hand_on(grads_in, kept_in, grads_out, kept_out, sem):
-    copies = [
-        pltpu.make_async_copy(kept_in, kept_out, sem.at[0]),
-        pltpu.make_async_copy(grads_in, grads_out, sem.at[1]),
-    ]
-    for copy in copies:
-        copy.start()
-    for copy in copies:
-        copy.wait()
+def hand_on(grads_in, kept_in, grads_out, kept_out):
+    grads_out[...] = grads_in[...]
+    kept_out[...] = kept_in[...]
 
 
 def shards(sections, section_inputs, top_gradient, gate_weight, up_weight, down_weight):
@@ -476,9 +469,8 @@
             jax.ShapeDtypeStruct(grads.shape, F32),
             jax.ShapeDtypeStruct(kept.shape, F32),
         ),
-        in_specs=[hbm, hbm],
-        out_specs=(hbm, hbm),
-        scratch_shapes=[dma((2,))],
+        in_specs=[vmem, vmem],
+        out_specs=(vmem, vmem),
     )(grads, kept)
     return (grads[None], kept[None])
 

time: 242 us -> 182 us (0.75)
  Pallas kernels: 241 us -> 181 us
    pallas_call x1, Pallas kernels: 59.7 us -> 2.91 us  [shards(): pl.pallas_call(hand_on, out_shape=(jax.ShapeDtypeStruct(grads.shape, F32)...]
    pallas_call x1, Pallas kernels: 182 us -> 178 us  [shards(): pl.pallas_call(functools.partial(kernel, sections, chips, rows, step_rows...]
where the time goes in v3:
time: 182 us
  Pallas kernels  181 us (99%)
    pallas_call x1, Pallas kernels, shards(): pl.pallas_call(functools.partial(kernel, sections, chips, rows, step_rows...  178 us

profile of v3, /device:TPU:1, one launch (start us, length us, event | category | flops | bytes accessed | tf_op | source)
XLA Modules:
  0.0 181.7 jit_solution(18051687734507386779)
XLA Ops:
  0.6 178.1 %shard_map.68 = (f32[192,128]{1,0:T(8,128)}, f32[112,4096]{1,0:T(8,128)}) custom-call(bf16[192,128]{1,0:T(8,128)(2,1)} %bitcast.13, f32[192,128]{1,0:T(8,128)} %top_ref.1, bf16[448,4096]{1,0:T(8,128)(2,1)} %bitcast.10, bf16[448,4096]{1,0:T(8,128)(2,1)} %bitcast.11, bf16[448,4096]{1,0:T(8,128)(2,1)} %bitcast.12), custom_call_target="tpu_custom_call" | custom-call | tf_op jit(solution)/shard_map/pallas_call | solution.py:419
  178.7 2.9 %shard_map.69 = (f32[192,128]{1,0:T(8,128)}, f32[112,4096]{1,0:T(8,128)}) custom-call(f32[192,128]{1,0:T(8,128)} %get-tuple-element.6.grads_in, f32[112,4096]{1,0:T(8,128)} %get-tuple-element.7.kept_in), custom_call_target="tpu_custom_call" | custom-call | tf_op jit(solution)/shard_map/pallas_call | solution.py:466

commit v4 on v3

--- a/solution.py
+++ b/solution.py
@@ -148,6 +148,16 @@
             ).start()
         pltpu.make_async_copy(top16.at[at], g_all.at[chip, at], gather_sem.at[step]).start()
 
+    for place in places[:-1]:
+        pltpu.make_async_remote_copy(
+            src_ref=x_ref,
+            dst_ref=x_all.at[chip],
+            send_sem=x_sem.at[0],
+            recv_sem=x_sem.at[1],
+            device_id=(section, 2 * place + core),
+            device_id_type=MESH,
+        ).start()
+    pltpu.make_async_copy(x_ref, x_all.at[chip], x_sem.at[1]).start()
     @pl.when(is_top)
     def _():
         spread_top(0)
@@ -162,16 +172,6 @@
                 device_id=sibling,
                 device_id_type=MESH,
             ).start()
-    for place in places[:-1]:
-        pltpu.make_async_remote_copy(
-            src_ref=x_ref,
-            dst_ref=x_all.at[chip],
-            send_sem=x_sem.at[0],
-            recv_sem=x_sem.at[1],
-            device_id=(section, 2 * place + core),
-            device_id_type=MESH,
-        ).start()
-    pltpu.make_async_copy(x_ref, x_all.at[chip], x_sem.at[1]).start()
     for k in range(chips):
         pltpu.make_async_remote_copy(
             src_ref=wd_hbm.at[:, columns_of(k, other)],
@@ -283,14 +283,14 @@
             ],
             axis=1,
         )
-        for pair in range(chips // 2):
+        for four in range(chips // 4):
             term = jnp.dot(
                 both,
-                both_t[:, :, :, pl.ds(2 * pair * CHUNK, 2 * CHUNK)].reshape(4 * units, 2 * CHUNK),
+                both_t[:, :, :, pl.ds(4 * four * CHUNK, 4 * CHUNK)].reshape(4 * units, 4 * CHUNK),
                 preferred_element_type=F32,
             ).astype(BF16)
-            for t in (2 * pair, 2 * pair + 1):
-                send_buf[t, at, :] = term[:, (t - 2 * pair) * CHUNK : (t - 2 * pair + 1) * CHUNK]
+            for t in range(4 * four, 4 * four + 4):
+                send_buf[t, at, :] = term[:, (t - 4 * four) * CHUNK : (t - 4 * four + 1) * CHUNK]
                 if t < chips - 1:
                     pltpu.make_async_remote_copy(
                         src_ref=send_buf.at[t, at],
@@ -327,11 +327,12 @@
 
     @pl.loop(0, steps)
     def _(step):
+        first(step)
+
         @pl.when(step >= lag)
         def _():
             third(step - lag)
 
-        first(step)
         second(step)
 
     @pl.loop(steps - lag, jnp.where(is_last, steps - lag, steps))

time: 182 us -> 163 us (0.90)
  Pallas kernels: 181 us -> 163 us
    pallas_call x1, Pallas kernels: 178 us -> 160 us  [shards(): pl.pallas_call(functools.partial(kernel, sections, chips, rows, step_rows...]
where the time goes in v4:
time: 163 us
  Pallas kernels  163 us (100%)
    pallas_call x1, Pallas kernels, shards(): pl.pallas_call(functools.partial(kernel, sections, chips, rows, step_rows...  160 us

profile of v4, /device:TPU:1, one launch (start us, length us, event | category | flops | bytes accessed | tf_op | source)
XLA Modules:
  0.0 163.2 jit_solution(16872094713555998891)
XLA Ops:
  0.6 159.6 %shard_map.68 = (f32[192,128]{1,0:T(8,128)}, f32[112,4096]{1,0:T(8,128)}) custom-call(bf16[192,128]{1,0:T(8,128)(2,1)} %bitcast.13, f32[192,128]{1,0:T(8,128)} %top_ref.1, bf16[448,4096]{1,0:T(8,128)(2,1)} %bitcast.10, bf16[448,4096]{1,0:T(8,128)(2,1)} %bitcast.11, bf16[448,4096]{1,0:T(8,128)(2,1)} %bitcast.12), custom_call_target="tpu_custom_call" | custom-call | tf_op jit(solution)/shard_map/pallas_call | solution.py:420
  160.3 2.9 %shard_map.69 = (f32[192,128]{1,0:T(8,128)}, f32[112,4096]{1,0:T(8,128)}) custom-call(f32[192,128]{1,0:T(8,128)} %get-tuple-element.6.grads_in, f32[112,4096]{1,0:T(8,128)} %get-tuple-element.7.kept_in), custom_call_target="tpu_custom_call" | custom-call | tf_op jit(solution)/shard_map/pallas_call | solution.py:467

commit v5 on v4

--- a/solution.py
+++ b/solution.py
@@ -56,8 +56,10 @@
     send_buf,
     recv_buf,
     part_mine,
+    part_send,
     part_other,
     pre_mine,
+    pre_send,
     pre_other,
     factor_gate,
     factor_up,
@@ -148,19 +150,30 @@
             ).start()
         pltpu.make_async_copy(top16.at[at], g_all.at[chip, at], gather_sem.at[step]).start()
 
-    for place in places[:-1]:
-        pltpu.make_async_remote_copy(
-            src_ref=x_ref,
-            dst_ref=x_all.at[chip],
-            send_sem=x_sem.at[0],
-            recv_sem=x_sem.at[1],
-            device_id=(section, 2 * place + core),
-            device_id_type=MESH,
-        ).start()
-    pltpu.make_async_copy(x_ref, x_all.at[chip], x_sem.at[1]).start()
+    first_rows = rows // SAMPLES
+    parts = (pl.ds(0, first_rows), pl.ds(first_rows, rows - first_rows))
+
+    def spread_x(part):
+        at = parts[part]
+        for place in places[:-1]:
+            pltpu.make_async_remote_copy(
+                src_ref=x_ref.at[at],
+                dst_ref=x_all.at[chip, at],
+                send_sem=x_sem.at[part],
+                recv_sem=x_sem.at[2 + part],
+                device_id=(section, 2 * place + core),
+                device_id_type=MESH,
+            ).start()
+        pltpu.make_async_copy(x_ref.at[at], x_all.at[chip, at], x_sem.at[2 + part]).start()
+
+    spread_x(0)
+
     @pl.when(is_top)
     def _():
         spread_top(0)
+        spread_top(1)
+
+    spread_x(1)
 
     for n, source in enumerate((wg_hbm, wu_hbm)):
         for t, place in enumerate(places):
@@ -184,29 +197,40 @@
 
     @pl.when(is_top)
     def _():
-        for step in range(1, steps):
+        for step in range(2, steps):
             spread_top(step)
 
     def wait(ref, sem):
         pltpu.make_async_copy(ref, ref, sem).wait()
 
-    wait(x_all, x_sem.at[1])
-    x_rows = jnp.concatenate([x_all[place] for place in places], axis=1)
-    for n in range(2):
-        wait(both_t.at[n, core], load_sem.at[n])
-        wait(both_t.at[n, other], swap_sem.at[3 + n])
-        for h in range(2):
-            pre_mine[n, h] = lax.dot_general(
-                x_rows, both_t[n, h], (((1,), (1,)), ((), ())), preferred_element_type=F32
-            )
-        pltpu.make_async_remote_copy(
-            src_ref=pre_mine.at[n],
-            dst_ref=pre_other.at[n],
-            send_sem=pre_sem.at[n],
-            recv_sem=pre_sem.at[2 + n],
-            device_id=sibling,
-            device_id_type=MESH,
-        ).start()
+    def forward_start(part):
+        at = parts[part]
+        wait(x_all.at[:, at], x_sem.at[2 + part])
+        x_rows = jnp.concatenate([x_all[place, at, :] for place in places], axis=1)
+        for n in range(2):
+            if part == 0:
+                wait(both_t.at[n, core], load_sem.at[n])
+                wait(both_t.at[n, other], swap_sem.at[3 + n])
+            for h in range(2):
+                partial = lax.dot_general(
+                    x_rows, both_t[n, h], (((1,), (1,)), ((), ())), preferred_element_type=F32
+                )
+                pre_mine[n, h, at, :] = partial
+                pre_send[n, h, at, :] = partial.astype(BF16)
+                pltpu.make_async_remote_copy(
+                    src_ref=pre_send.at[n, h, at],
+                    dst_ref=pre_other.at[n, h, at],
+                    send_sem=pre_sem.at[0, part, 2 * n + h],
+                    recv_sem=pre_sem.at[1, part, 2 * n + h],
+                    device_id=sibling,
+                    device_id_type=MESH,
+                ).start()
+
+    forward_start(0)
+
+    @pl.when(jnp.logical_not(is_top))
+    def _():
+        forward_start(1)
 
     wait(w_down.at[core], load_sem.at[2])
     wait(w_down.at[other], swap_sem.at[5])
@@ -224,29 +248,6 @@
     )
     spread = (from_unit == 4 * (to_place - member * fourth) + member).astype(F32).astype(BF16)
 
-    wait(pre_other.at[0], pre_sem.at[2])
-    wait(pre_other.at[1], pre_sem.at[3])
-    gates, ups = [], []
-    for h in range(2):
-        pre_gate = pre_mine[0, h] + pre_other[0, h]
-        pre_up = pre_mine[1, h] + pre_other[1, h]
-        sigmoid = jax.nn.sigmoid(pre_gate)
-        silu = pre_gate * sigmoid
-        gates.append(pre_up * (sigmoid * (1.0 + pre_gate * (1.0 - sigmoid))))
-        ups.append(silu)
-        hidden = (silu * pre_up).astype(BF16)
-
-        @pl.when(core == h)
-        def _():
-            for sample in range(SAMPLES):
-                some = hidden[sample * (rows // SAMPLES) : (sample + 1) * (rows // SAMPLES)]
-                hidden_t[sample] = lax.dot_general(
-                    spread, some, (((1,), (1,)), ((), ())), preferred_element_type=F32
-                ).astype(BF16)
-
-    factor_gate[...] = jnp.concatenate(gates, axis=1)
-    factor_up[...] = jnp.concatenate(ups, axis=1)
-
     def rows_of(step):
         return pl.ds(pl.multiple_of(step * step_rows, step_rows), step_rows)
 
@@ -254,9 +255,11 @@
         at = rows_of(step)
         wait(g_all.at[:, at], gather_sem.at[step])
         grads = jnp.concatenate([g_all[k, at, :] for k in range(chips)], axis=1)
-        part_mine[at, :] = jnp.dot(grads, down_t[...], preferred_element_type=F32)
+        partial = jnp.dot(grads, down_t[...], preferred_element_type=F32)
+        part_mine[at, :] = partial
+        part_send[at, :] = partial.astype(BF16)
         pltpu.make_async_remote_copy(
-            src_ref=part_mine.at[at],
+            src_ref=part_send.at[at],
             dst_ref=part_other.at[at],
             send_sem=part_sem.at[0, step],
             recv_sem=part_sem.at[1, step],
@@ -275,7 +278,7 @@
     def second(step):
         at = rows_of(step)
         wait(part_other.at[at], part_sem.at[1, step])
-        hidden_grad = part_mine[at, :] + part_other[at, :]
+        hidden_grad = part_mine[at, :] + part_other[at, :].astype(F32)
         both = jnp.concatenate(
             [
                 (hidden_grad * factor_gate[at, :]).astype(BF16),
@@ -323,17 +326,64 @@
                     device_id_type=MESH,
                 ).start()
 
+    @pl.when(is_top)
+    def _():
+        first(0)
+
+    def forward_end(part):
+        at = parts[part]
+        gates, ups = [], []
+        for h in range(2):
+            wait(pre_other.at[0, h, at], pre_sem.at[1, part, h])
+            wait(pre_other.at[1, h, at], pre_sem.at[1, part, 2 + h])
+            pre_gate = pre_mine[0, h, at, :] + pre_other[0, h, at, :].astype(F32)
+            pre_up = pre_mine[1, h, at, :] + pre_other[1, h, at, :].astype(F32)
+            sigmoid = jax.nn.sigmoid(pre_gate)
+            silu = pre_gate * sigmoid
+            gates.append(pre_up * (sigmoid * (1.0 + pre_gate * (1.0 - sigmoid))))
+            ups.append(silu)
+            hidden = (silu * pre_up).astype(BF16)
+
+            @pl.when(core == h)
+            def _():
+                for n, sample in enumerate(((0,), range(1, SAMPLES))[part]):
+                    hidden_t[sample] = lax.dot_general(
+                        spread,
+                        hidden[n * first_rows : (n + 1) * first_rows],
+                        (((1,), (1,)), ((), ())),
+                        preferred_element_type=F32,
+                    ).astype(BF16)
+
+        factor_gate[at, :] = jnp.concatenate(gates, axis=1)
+        factor_up[at, :] = jnp.concatenate(ups, axis=1)
+
+    forward_end(0)
+
+    @pl.when(jnp.logical_not(is_top))
+    def _():
+        forward_end(1)
+
     lag = 2
 
     @pl.loop(0, steps)
     def _(step):
-        first(step)
+        @pl.when(jnp.logical_or(step > 0, jnp.logical_not(is_top)))
+        def _():
+            first(step)
 
         @pl.when(step >= lag)
         def _():
             third(step - lag)
 
+        @pl.when(jnp.logical_and(is_top, step == lag))
+        def _():
+            forward_end(1)
+
         second(step)
+
+        @pl.when(jnp.logical_and(is_top, step == lag - 1))
+        def _():
+            forward_start(1)
 
     @pl.loop(steps - lag, jnp.where(is_last, steps - lag, steps))
     def _(step):
@@ -382,14 +432,16 @@
     wait(both_t.at[0, core], swap_sem.at[0])
     wait(both_t.at[1, core], swap_sem.at[1])
     wait(w_down.at[core], swap_sem.at[2])
-    wait(x_all.at[pl.ds(0, chips - 1)], x_sem.at[0])
-    wait(pre_mine.at[0], pre_sem.at[0])
-    wait(pre_mine.at[1], pre_sem.at[1])
+    for part, at in enumerate(parts):
+        wait(x_all.at[pl.ds(0, chips - 1), at], x_sem.at[part])
+        for n in range(2):
+            for h in range(2):
+                wait(pre_send.at[n, h, at], pre_sem.at[0, part, 2 * n + h])
 
     @pl.loop(0, steps)
     def _(step):
         at = rows_of(step)
-        wait(part_mine.at[at], part_sem.at[0, step])
+        wait(part_send.at[at], part_sem.at[0, step])
         wait(g_all.at[:, at], forward_sem.at[0, step])
         wait(recv_buf.at[:, at], term_sem.at[0, step])
 
@@ -438,16 +490,18 @@
             pltpu.VMEM((chips, rows, CHUNK), BF16),
             pltpu.VMEM((chips - 1, rows, CHUNK), BF16),
             pltpu.VMEM((rows, 2 * units), F32),
-            pltpu.VMEM((rows, 2 * units), F32),
+            pltpu.VMEM((rows, 2 * units), BF16),
+            pltpu.VMEM((rows, 2 * units), BF16),
             pltpu.VMEM((2, 2, rows, units), F32),
-            pltpu.VMEM((2, 2, rows, units), F32),
+            pltpu.VMEM((2, 2, rows, units), BF16),
+            pltpu.VMEM((2, 2, rows, units), BF16),
             pltpu.VMEM((rows, 2 * units), F32),
             pltpu.VMEM((rows, 2 * units), F32),
             pltpu.VMEM((SAMPLES, units, rows // SAMPLES), BF16),
             dma((4,)),
             dma((6,)),
-            dma((2,)),
             dma((4,)),
+            dma((2, 2, 4)),
             dma((steps,)),
             dma((2 * steps,)),
             dma((2, steps)),

time: 163 us -> 160 us (0.982)
  Pallas kernels: 163 us -> 159 us
    pallas_call x1, Pallas kernels: 160 us -> 156 us  [shards(): pl.pallas_call(functools.partial(kernel, sections, chips, rows, step_rows...]
where the time goes in v5:
time: 160 us
  Pallas kernels  159 us (99%)
    pallas_call x1, Pallas kernels, shards(): pl.pallas_call(functools.partial(kernel, sections, chips, rows, step_rows...  156 us

profile of v5, /device:TPU:1, one launch (start us, length us, event | category | flops | bytes accessed | tf_op | source)
XLA Modules:
  0.0 159.7 jit_solution(15423641951396147381)
XLA Ops:
  0.6 156.2 %shard_map.68 = (f32[192,128]{1,0:T(8,128)}, f32[112,4096]{1,0:T(8,128)}) custom-call(bf16[192,128]{1,0:T(8,128)(2,1)} %bitcast.13, f32[192,128]{1,0:T(8,128)} %top_ref.1, bf16[448,4096]{1,0:T(8,128)(2,1)} %bitcast.10, bf16[448,4096]{1,0:T(8,128)(2,1)} %bitcast.11, bf16[448,4096]{1,0:T(8,128)(2,1)} %bitcast.12), custom_call_target="tpu_custom_call" | custom-call | tf_op jit(solution)/shard_map/pallas_call | solution.py:472
  156.8 2.9 %shard_map.69 = (f32[192,128]{1,0:T(8,128)}, f32[112,4096]{1,0:T(8,128)}) custom-call(f32[192,128]{1,0:T(8,128)} %get-tuple-element.6.grads_in, f32[112,4096]{1,0:T(8,128)} %get-tuple-element.7.kept_in), custom_call_target="tpu_custom_call" | custom-call | tf_op jit(solution)/shard_map/pallas_call | solution.py:521

commit v6 on v5

--- a/solution.py
+++ b/solution.py
@@ -266,14 +266,6 @@
             device_id=sibling,
             device_id_type=MESH,
         ).start()
-        pltpu.make_async_remote_copy(
-            src_ref=g_all.at[:, at],
-            dst_ref=g_other.at[:, at],
-            send_sem=forward_sem.at[0, step],
-            recv_sem=forward_sem.at[1, step],
-            device_id=sibling,
-            device_id_type=MESH,
-        ).start()
 
     def second(step):
         at = rows_of(step)
@@ -304,6 +296,17 @@
                         device_id_type=MESH,
                     ).start()
 
+    def pass_on(step):
+        at = rows_of(step)
+        pltpu.make_async_remote_copy(
+            src_ref=g_all.at[:, at],
+            dst_ref=g_other.at[:, at],
+            send_sem=forward_sem.at[0, step],
+            recv_sem=forward_sem.at[1, step],
+            device_id=sibling,
+            device_id_type=MESH,
+        ).start()
+
     def third(step):
         at = rows_of(step)
         wait(recv_buf.at[:, at], term_sem.at[1, step])
@@ -380,6 +383,7 @@
             forward_end(1)
 
         second(step)
+        pass_on(step)
 
         @pl.when(jnp.logical_and(is_top, step == lag - 1))
         def _():

time: 160 us -> 161 us (level)
  no operation moved by 1% of the time
where the time goes in v6:
time: 161 us
  Pallas kernels  160 us (99%)
    pallas_call x1, Pallas kernels, shards(): pl.pallas_call(functools.partial(kernel, sections, chips, rows, step_rows...  158 us

profile of v6, /device:TPU:1, one launch (start us, length us, event | category | flops | bytes accessed | tf_op | source)
XLA Modules:
  0.0 161.1 jit_solution(15781377912204384111)
XLA Ops:
  0.6 157.5 %shard_map.68 = (f32[192,128]{1,0:T(8,128)}, f32[112,4096]{1,0:T(8,128)}) custom-call(bf16[192,128]{1,0:T(8,128)(2,1)} %bitcast.13, f32[192,128]{1,0:T(8,128)} %top_ref.1, bf16[448,4096]{1,0:T(8,128)(2,1)} %bitcast.10, bf16[448,4096]{1,0:T(8,128)(2,1)} %bitcast.11, bf16[448,4096]{1,0:T(8,128)(2,1)} %bitcast.12), custom_call_target="tpu_custom_call" | custom-call | tf_op jit(solution)/shard_map/pallas_call | solution.py:476
  158.1 2.9 %shard_map.69 = (f32[192,128]{1,0:T(8,128)}, f32[112,4096]{1,0:T(8,128)}) custom-call(f32[192,128]{1,0:T(8,128)} %get-tuple-element.6.grads_in, f32[112,4096]{1,0:T(8,128)} %get-tuple-element.7.kept_in), custom_call_target="tpu_custom_call" | custom-call | tf_op jit(solution)/shard_map/pallas_call | solution.py:525
